TPU v7x, 32 devices: a whole 2x2x4 slice. The times are simulated.
32 devices in a mesh: groups: 2 (over y), ctx: 4 (over z), dp: 4 (over x, core).
Axes of the slice: x: 2, y: 2, z: 4, core: 2. Of those that a mesh axis runs over, the one named last changes fastest.
Arguments:
- values: bfloat16 [8, 512, 1024], P(('groups', 'dp'), 'ctx'), parts along dimension 0, may hold values from -6 to 6
- grads_out: bfloat16 [8, 512, 1024], P(('groups', 'dp'), 'ctx'), parts along dimension 0, may hold values from -6 to 6
- w_first: float32 [5, 64], replicated, may hold values from -2.5 to 2.5
- sine_freq: float32 [64], replicated, may hold values from 0.5 to 2
- w_inner: float32 [64, 64], replicated, may hold values from -0.75 to 0.75
- w_last: float32 [64, 1024], replicated, may hold values from -0.75 to 0.75
- decay_rates: float32 [1024], replicated, may hold values from 6e-05 to 0.03
Outputs:
- grad_first: float32 [10, 64], P('groups'), parts along dimension 0
- grad_inner: float32 [128, 64], P('groups'), parts along dimension 0
- grad_last: float32 [128, 1024], P('groups'), parts along dimension 0
There are 2 independent parts, one for each index of `groups`. A program takes and returns all parts, laid end to end along the dimension named above; an argument that names none is the same for every part. Nothing has to cross between parts.
All inputs are finite; a program needn't handle non-finite values.
Results may differ from a plain program's by a relative error of at most 0.0003.
Values may be sent and summed in bfloat16 or wider, within the bound.
A program may use at most 64 MiB of HBM per device.

v0:
```python
import math

import jax
import jax.numpy as jnp
from jax import lax
from jax.sharding import PartitionSpec as P

L = 4096


HIGHEST_PREC = lax.Precision.HIGHEST


def shifted(value, axis, steps):
    count = lax.axis_size(axis)
    initial, last = (max(0, -steps), min(count, count - steps))
    return lax.ppermute(value, axis, [(source, source + steps) for source in range(initial, last)])


def position_features(row_count, lag_total):
    positions = jnp.arange(row_count, dtype=jnp.int32)
    columns = [positions.astype(jnp.float32) / lag_total]
    for band_idx in (1, 2):
        phase_idx = positions * band_idx % lag_total
        angles = 2.0 * math.pi * phase_idx.astype(jnp.float32) / lag_total
        columns.append(jnp.cos(angles))
        columns.append(jnp.sin(angles))
    return jnp.stack(columns, axis=1)


def filter_forward(features, w_first, w_inner, sine_freq):
    pre_first = jnp.dot(
        features, w_first, precision=HIGHEST_PREC, preferred_element_type=jnp.float32
    )
    act_first = jnp.sin(sine_freq * pre_first)
    pre_inner = jnp.dot(
        act_first, w_inner, precision=HIGHEST_PREC, preferred_element_type=jnp.float32
    )
    act_inner = jnp.sin(sine_freq * pre_inner)
    return (pre_first, act_first, pre_inner, act_inner)


def filter_back(features, pre_first, act_first, pre_inner, grad_act, w_inner, sine_freq):
    grad_pre = grad_act * sine_freq * jnp.cos(sine_freq * pre_inner)
    grad_inner = jnp.dot(
        act_first.T, grad_pre, precision=HIGHEST_PREC, preferred_element_type=jnp.float32
    )
    grad_act_first = jnp.dot(
        grad_pre, w_inner.T, precision=HIGHEST_PREC, preferred_element_type=jnp.float32
    )
    grad_pre_first = grad_act_first * sine_freq * jnp.cos(sine_freq * pre_first)
    grad_first = jnp.dot(
        features.T, grad_pre_first, precision=HIGHEST_PREC, preferred_element_type=jnp.float32
    )
    return (grad_first, grad_inner)


def spectral_tables(block_len):
    full_len = 2 * block_len
    freq_idx = jnp.arange(block_len, dtype=jnp.int32)
    places = jnp.arange(full_len, dtype=jnp.int32)
    phase_idx = freq_idx[:, None] * places[None, :] % full_len
    angles = math.pi * phase_idx.astype(jnp.float32) / block_len
    back_phase = freq_idx[:, None] * freq_idx[None, :] % full_len
    back_angles = math.pi * back_phase.astype(jnp.float32) / block_len
    weights = jnp.where(freq_idx == 0, 1.0, 2.0).astype(jnp.float32) / full_len
    inv_cos = jnp.cos(back_angles) * weights[None, :]
    inv_sin = jnp.sin(back_angles) * weights[None, :]
    parity = 1.0 - 2.0 * (places % 2).astype(jnp.float32)
    return (jnp.cos(angles), jnp.sin(angles), inv_cos, inv_sin, parity)


def spectrum(cos_part, sin_part, sign_part, signal):
    real_part = jnp.einsum("fn,bnc->bfc", cos_part, signal, precision=HIGHEST_PREC)
    imag_part = -jnp.einsum("fn,bnc->bfc", sin_part, signal, precision=HIGHEST_PREC)
    nyquist = jnp.einsum("n,bnc->bc", sign_part, signal, precision=HIGHEST_PREC)
    return (real_part, imag_part, nyquist)


def lag_block_update(carried, pieces, block_idx, own_spec, shared):
    grad_act, grad_last = carried
    tables, act_inner, w_last, decay_rates, grad_scale = shared
    fwd_cos, fwd_sin, inv_cos, inv_sin, parity = tables
    block_len = inv_cos.shape[0]
    blocks = act_inner.shape[0] // block_len
    own_real, own_imag, own_nyq = own_spec
    in_real, in_imag, in_nyq = spectrum(
        fwd_cos[:, block_len:],
        fwd_sin[:, block_len:],
        parity[block_len:],
        pieces.astype(jnp.float32),
    )
    cross_real = jnp.sum(in_real * own_real + in_imag * own_imag, axis=0)
    cross_imag = jnp.sum(in_imag * own_real - in_real * own_imag, axis=0)
    cross_nyq = jnp.sum(in_nyq * own_nyq, axis=0)
    lagged = jnp.dot(
        inv_cos, cross_real, precision=HIGHEST_PREC, preferred_element_type=jnp.float32
    )
    lagged = lagged - jnp.dot(
        inv_sin, cross_imag, precision=HIGHEST_PREC, preferred_element_type=jnp.float32
    )
    lagged = lagged + (parity[:block_len] / (2 * block_len))[:, None] * cross_nyq[None, :]
    in_range = (block_idx >= 0) & (block_idx < blocks)
    row_start = jnp.clip(block_idx, 0, blocks - 1) * block_len
    lag_pos = (row_start + jnp.arange(block_len, dtype=jnp.int32)).astype(jnp.float32)
    window = jnp.exp(-lag_pos[:, None] * decay_rates[None, :])
    cotangent = jnp.where(in_range, lagged * window * grad_scale, 0.0)
    act_rows = lax.dynamic_slice_in_dim(act_inner, row_start, block_len, 0)
    grad_last = grad_last + jnp.dot(
        act_rows.T, cotangent, precision=HIGHEST_PREC, preferred_element_type=jnp.float32
    )
    current = lax.dynamic_slice_in_dim(grad_act, row_start, block_len, 0)
    update = jnp.dot(
        cotangent, w_last.T, precision=HIGHEST_PREC, preferred_element_type=jnp.float32
    )
    grad_act = lax.dynamic_update_slice_in_dim(grad_act, current + update, row_start, 0)
    return (grad_act, grad_last)


def shards(values, grads_out, w_first, sine_freq, w_inner, w_last, decay_rates):
    block_len = values.shape[1]
    lag_total = L
    tables = spectral_tables(block_len)
    fwd_cos, fwd_sin, inv_cos, inv_sin, parity = tables
    token_count = (
        values.shape[0] * lax.axis_size("dp") * block_len * lax.axis_size("ctx") * lag_total
    )
    grad_scale = 1.0 / math.sqrt(token_count)
    features = position_features(lag_total, lag_total)
    pre_first, act_first, pre_inner, act_inner = filter_forward(
        features, w_first, w_inner, sine_freq
    )
    earlier = shifted(values, "ctx", 1)
    own_pair = jnp.concatenate([earlier, values], axis=1).astype(jnp.float32)
    own_spec = spectrum(fwd_cos, fwd_sin, parity, own_pair)
    shared = (tables, act_inner, w_last, decay_rates, grad_scale)
    carried = (
        jnp.zeros((lag_total, w_last.shape[0]), jnp.float32),
        jnp.zeros(w_last.shape, jnp.float32),
    )
    ctx_index = lax.axis_index("ctx")
    pieces = lax.all_gather(grads_out[None], "ctx", axis=0, tiled=True)

    def one_piece(piece_idx, piece_state):
        return lag_block_update(
            piece_state, pieces[piece_idx], piece_idx - ctx_index, own_spec, shared
        )

    carried = lax.fori_loop(0, pieces.shape[0], one_piece, carried)
    grad_act, grad_last = carried
    grad_act, grad_last = lax.psum((grad_act, grad_last), ("ctx", "dp"))
    grad_first, grad_inner = filter_back(
        features, pre_first, act_first, pre_inner, grad_act, w_inner, sine_freq
    )
    return (grad_first, grad_inner, grad_last)


def solution(mesh):
    in_specs = (
        P(("groups", "dp"), "ctx", None),
        P(("groups", "dp"), "ctx", None),
        P(),
        P(),
        P(),
        P(),
        P(),
    )
    out_specs = (P("groups", None), P("groups", None), P("groups", None))
    return jax.shard_map(shards, mesh=mesh, in_specs=in_specs, out_specs=out_specs, check_vma=False)
```

profile of v0, /device:TPU:0, one launch (start us, length us, event | category | flops | bytes accessed | tf_op | source)
XLA Modules:
  0.0 188.5 jit_solution(17585985129269242798)
XLA Ops:
  7.2 0.7 all-gather.3.cloned.1.call-update
  8.1 4.9 %collective-permute-start = (bf16[1,128,1024]{2,1,0:T(8,128)(2,1)S(1)}, bf16[1,128,1024]{2,1,0:T(8,128)(2,1)S(1)}, u32[]{:S(2)}, u32[]{:S(2)}) collective-permute-start(bf16[1,128,1024]{2,1,0:T(8,128)(2,1)S(1)} %copy-done.15), channel_id=1, source_target_pairs={{0,4},{4,8},{8,12},{1,5},{5,9},{9,13},{2,6},{6,10},{10,14},{3,7},{... | collective-permute-start | bytes 786440 | tf_op jit(solution)/shard_map/ppermute | solution.py:17
  13.1 0.9 fusion.78
  14.0 0.5 convert_multiply_fusion
  14.5 0.4 fusion.80
  15.2 1.2 fusion.68
  16.4 5.7 %fusion.96 = (f32[4096,64]{0,1:T(8,128)S(1)}, f32[4096,64]{0,1:T(8,128)}) fusion(f32[4096,5]{0,1:T(8,128)S(1)} %stack.2, f32[5,64]{1,0:T(8,128)S(1)} %copy-done.14, f32[64]{0:T(128)S(1)} %copy-done.13), kind=kOutput, calls=%fused_computation.117 | convolution fusion | flops 15990784 | bytes 2180608 | tf_op jit(solution)/shard_map/dot_general | solution.py:32
  22.1 5.8 %fusion.97 = (f32[4096,64]{0,1:T(8,128)}, f32[4096,64]{0,1:T(8,128)}) fusion(f32[4096,64]{0,1:T(8,128)S(1)} %get-tuple-element.496, f32[64,64]{1,0:T(8,128)S(1)} %copy-done, f32[64]{0:T(128)S(1)} %copy-done.13), kind=kOutput, calls=%fused_computation.118 | convolution fusion | flops 201588736 | bytes 3162368 | tf_op jit(solution)/shard_map/dot_general | solution.py:36
  28.0 1.1 convolution_bitcast_fusion.1
  29.1 1.1 fusion.59
  30.6 9.6 %all-gather.3.cloned.1.call-done = bf16[4,128,1024]{2,1,0:T(8,128)(2,1)} async-done(((bf16[1,128,1024]{2,1,0:T(8,128)(2,1)}), bf16[4,128,1024]{2,1,0:T(8,128)(2,1)}) %all-gather.3.cloned.1.call-update) | async-done | bytes 1048592 | tf_op jit(solution)/shard_map/all_gather | solution.py:142
  40.2 1.1 broadcast_in_dim.49
  41.3 0.5 copy-done.1
  41.8 29.4 %while.19 = (s32[]{:T(128)}, f32[4096,64]{0,1:T(8,128)}, f32[64,1024]{1,0:T(8,128)S(1)}, s32[]{:T(128)}, bf16[4,1,128,1024]{3,2,1,0:T(8,128)(2,1)S(1)}, /*index=...) while((s32[]{:T(128)}, f32[4096,64]{0,1:T(8,128)}, ...), condition=%wide.region_1.2_spmd.clone.clone.clone.clone, body=%wide.region_0.1_spmd.clone.clone.clone.clone.sunk | while | flops 1010673152 | bytes 11792803 | solution.py:149
  42.0 0.7 copy-done.7
  42.7 0.4 fusion.144
  43.1 0.5 copy-done.8
  44.0 0.8 fusion.145
  44.9 0.9 fusion.147
  45.8 1.5 convolution_add_fusion.3
  47.3 1.8 fusion.148
  49.3 0.7 copy-done.7
  50.0 0.4 fusion.144
  50.5 0.5 copy-done.8
  51.4 0.8 fusion.145
  52.2 0.9 fusion.147
  53.1 1.5 convolution_add_fusion.3
  54.6 1.8 fusion.148
  56.7 0.7 copy-done.7
  57.4 0.4 fusion.144
  57.8 0.5 copy-done.8
  58.7 0.8 fusion.145
  59.6 0.9 fusion.147
  60.5 1.5 convolution_add_fusion.3
  62.0 1.8 fusion.148
  64.0 0.7 copy-done.7
  64.7 0.4 fusion.144
  65.2 0.5 copy-done.8
  66.1 0.8 fusion.145
  66.9 0.9 fusion.147
  67.8 1.5 convolution_add_fusion.3
  69.3 1.8 fusion.148
  71.2 0.7 copy-done.2
  71.9 93.5 %all-reduce.3.cloned.1.call-done = (f32[4096,64]{0,1:T(8,128)}, f32[64,1024]{1,0:T(8,128)}) async-done(((f32[4096,64]{0,1:T(8,128)}, f32[64,1024]{1,0:T(8,128)}), (f32[4096,64]{0,1:T(8,128)}, f32[64,1024]{1,0:T(8,128)})) %all-reduce.3.cloned.1.call-update) | async-done | bytes 1310736 | tf_op jit(solution)/shard_map/psum | solution.py:151
  165.3 6.3 %fusion.67 = f32[64,64]{1,0:T(8,128)} fusion(f32[4096,64]{0,1:T(8,128)S(1)} %get-tuple-element.496, f32[4096,64]{0,1:T(8,128)S(1)} %copy-done.3, f32[4096,64]{0,1:T(8,128)} %get-tuple-element.492, f32[64]{0:T(128)S(1)} %copy-done.13), kind=kOutput, calls=%fused_computation.83 | convolution fusion | flops 201850880 | bytes 3162368 | tf_op jit(solution)/shard_map/dot_general | solution.py:45
  171.7 7.7 %fusion.58 = f32[4096,64]{0,1:T(8,128)S(1)} fusion(f32[64,64]{1,0:T(8,128)S(1)} %copy-done, f32[4096,64]{0,1:T(8,128)S(1)} %copy-done.5, f32[64]{0:T(128)S(1)} %copy-done.13, f32[4096,64]{0,1:T(8,128)S(1)} %copy-done.3, f32[4096,64]{0,1:T(8,128)S(1)} %copy-done.6), kind=kOutput, calls=%fused_computation.65 | convolution fusion | flops 202375168 | bytes 4210944 | tf_op jit(solution)/shard_map/dot_general | solution.py:48
  179.4 1.5 fusion.98
  180.9 0.7 copy.26
  (65 shorter events, 3.5 us)
Async XLA Ops:
  7.2 15.0 %copy-start = (f32[64,64]{1,0:T(8,128)S(1)}, f32[64,64]{1,0:T(8,128)}, u32[]{:S(2)}) copy-start(f32[64,64]{1,0:T(8,128)} %param.13) | copy-start | bytes 49156
  7.2 1.0 copy-start.15
  7.2 33.0 %all-gather.3.cloned.1.call-start = ((), (), s32[]{:S(2)}) async-start(), calls=%async_computation | async-start | bytes 1310720 | tf_op jit(solution)/shard_map/all_gather | solution.py:142
  7.9 157.4 %all-reduce.3.cloned.1.call-start = ((), (), s32[]{:S(2)}) async-start(), calls=%async_computation.1 | async-start | bytes 2621440 | tf_op jit(solution)/shard_map/psum | solution.py:151
  8.1 19.8 %collective-permute-start = (bf16[1,128,1024]{2,1,0:T(8,128)(2,1)S(1)}, bf16[1,128,1024]{2,1,0:T(8,128)(2,1)S(1)}, u32[]{:S(2)}, u32[]{:S(2)}) collective-permute-start(bf16[1,128,1024]{2,1,0:T(8,128)(2,1)S(1)} %copy-done.15), channel_id=1, source_target_pairs={{0,4},{4,8},{8,12},{1,5},{5,9},{9,13},{2,6},{6,10},{10,14},{3,7},{... | collective-permute-start | bytes 786440 | tf_op jit(solution)/shard_map/ppermute | solution.py:17
  15.1 1.3 copy-start.9
  15.1 1.3 copy-start.13
  15.2 1.3 copy-start.14
  40.2 1.6 copy-start.1
  40.2 1.6 copy-start.12
  41.8 0.9 copy-start.7
  42.7 0.9 copy-start.8
  45.7 1.5 copy-start.4
  49.1 0.9 copy-start.7
  50.0 0.9 copy-start.8
  53.1 1.5 copy-start.4
  56.5 0.9 copy-start.7
  57.4 0.9 copy-start.8
  60.4 1.5 copy-start.4
  63.8 0.9 copy-start.7
  64.7 0.9 copy-start.8
  67.8 1.5 copy-start.4
  71.1 0.7 copy-start.2
  71.1 94.2 %copy-start.3 = (f32[4096,64]{0,1:T(8,128)S(1)}, f32[4096,64]{0,1:T(8,128)}, u32[]{:S(2)}) copy-start(f32[4096,64]{0,1:T(8,128)} %get-tuple-element.499) | copy-start | bytes 3145732
  165.3 6.4 %copy-start.5 = (f32[4096,64]{0,1:T(8,128)S(1)}, f32[4096,64]{0,1:T(8,128)}, u32[]{:S(2)}) copy-start(f32[4096,64]{0,1:T(8,128)} %get-tuple-element.497) | copy-start | bytes 3145732
  165.3 6.4 %copy-start.6 = (f32[4096,64]{0,1:T(8,128)S(1)}, f32[4096,64]{0,1:T(8,128)}, u32[]{:S(2)}) copy-start(f32[4096,64]{0,1:T(8,128)} %get-tuple-element.492) | copy-start | bytes 3145732
  171.7 7.7 %copy-start.10 = (f32[4096,5]{0,1:T(8,128)S(1)}, f32[4096,5]{0,1:T(8,128)}, u32[]{:S(2)}) copy-start(f32[4096,5]{0,1:T(8,128)} %copy-done.9) | copy-start | bytes 245764
  179.4 1.5 copy-start.11
Sparse Core Ops, SparseCore 0:
  9.6 30.5 all-gather.2
  72.0 93.2 all-reduce.2
where the time goes:
time: 189 us; the launch traced here: 188 us
  waiting for transfers between devices  104 us (55%)
  matrix products  54.2 us (29%)
  between operations  14.2 us (8%)
  local copies, waits for them, and re-layouts  7.91 us (4%)
  starting transfers between devices  5.01 us (3%)
  other arithmetic  3.18 us (2%)
    psum x1, waiting for transfers between devices, shards(): grad_act, grad_last = lax.psum((grad_act, grad_last), ('ctx', 'dp'))  93.5 us
    all_gather x1, waiting for transfers between devices, shards(): pieces = lax.all_gather(grads_out[None], 'ctx', axis=0, tiled=True)  9.57 us
    dot_general x1, matrix products, filter_back(): jnp.dot(grad_pre, w_inner.T, precision=HIGHEST_PREC, preferred_element_ty...  7.67 us
    dot_general x4, matrix products, lag_block_update(): jnp.dot(cotangent, w_last.T, precision=HIGHEST_PREC, preferred_element_ty...  7.32 us
    dot_general x1, matrix products, filter_back(): jnp.dot(act_first.T, grad_pre, precision=HIGHEST_PREC, preferred_element_...  6.35 us
    dot_general x4, matrix products, lag_block_update(): jnp.dot(act_rows.T, cotangent, precision=HIGHEST_PREC, preferred_element_...  5.99 us
    dot_general x1, matrix products, filter_forward(): jnp.dot(act_first, w_inner, precision=HIGHEST_PREC, preferred_element_typ...  5.85 us
    dot_general x1, matrix products, filter_forward(): jnp.dot(features, w_first, precision=HIGHEST_PREC, preferred_element_type...  5.69 us
  transfers between devices with their start and end apart: 3, of which 2 were waited for; matrix products, arithmetic and copies ran while one was open for 9% of the time, Pallas kernels for 0%

commit v1 on v0

--- a/solution.py
+++ b/solution.py
@@ -1,8 +1,13 @@
+import functools
 import math
 
 import jax
 import jax.numpy as jnp
+import ml_dtypes
+import numpy as np
 from jax import lax
+from jax.experimental import pallas as pl
+from jax.experimental.pallas import tpu as pltpu
 from jax.sharding import PartitionSpec as P
 
 L = 4096
@@ -155,6 +160,288 @@
     return (grad_first, grad_inner, grad_last)
 
 
+MESH = pl.DeviceIdType.MESH
+FREQ_ROWS = 128
+
+
+def split_bf16(array):
+    high = array.astype(jnp.bfloat16)
+    return high, (array - high.astype(jnp.float32)).astype(jnp.bfloat16)
+
+
+def half_step_tables(total):
+    freq = np.arange(total, dtype=np.int64)
+    place = np.arange(total, dtype=np.int64)
+    phase = ((2 * freq[:, None] + 1) * place[None, :]) % (4 * total)
+    angle = np.pi * phase / (2 * total)
+    chunks = total // FREQ_ROWS
+    cos_part = np.cos(angle).reshape(chunks, FREQ_ROWS, total)
+    sin_part = np.sin(angle).reshape(chunks, FREQ_ROWS, total)
+    table = np.concatenate([cos_part, sin_part], axis=1).astype(np.float32)
+    high = table.astype(ml_dtypes.bfloat16)
+    low = (table - high.astype(np.float32)).astype(ml_dtypes.bfloat16)
+    flip = lambda part: np.ascontiguousarray(part.transpose(0, 2, 1))
+    return high, low, flip(high), flip(low)
+
+
+def feature_rows(total, rows):
+    place = np.arange(total, dtype=np.int64)
+    out = np.zeros((rows, total), np.float32)
+    out[0] = place / L
+    for band in (1, 2):
+        angle = 2.0 * np.pi * (place * band % L) / L
+        out[2 * band - 1] = np.cos(angle)
+        out[2 * band] = np.sin(angle)
+    return out
+
+
+def sin_cos(x):
+    turns = jnp.floor(x * np.float32(2.0 / np.pi) + 0.5)
+    r = x - turns * np.float32(1.5703125)
+    r = r - turns * np.float32(4.837512969970703125e-4)
+    r = r - turns * np.float32(7.54978995489188216e-8)
+    z = r * r
+    s = ((np.float32(-1.9515295891e-4) * z + np.float32(8.3321608736e-3)) * z
+         + np.float32(-1.6666654611e-1)) * z * r + r
+    c = ((np.float32(2.443315711809948e-5) * z + np.float32(-1.388731625493765e-3)) * z
+         + np.float32(4.166664568298827e-2)) * z * z - 0.5 * z + 1.0
+    quarter = turns - 4.0 * jnp.floor(turns * 0.25)
+    odd = (quarter == 1.0) | (quarter == 3.0)
+    sin_flip = jnp.where(quarter >= 2.0, -1.0, 1.0)
+    cos_flip = jnp.where((quarter == 1.0) | (quarter == 2.0), -1.0, 1.0)
+    return jnp.where(odd, c, s) * sin_flip, jnp.where(odd, s, c) * cos_flip
+
+
+def dot(a, b, dims=((1,), (0,)), precision=None):
+    return lax.dot_general(
+        a, b, (dims, ((), ())), precision=precision, preferred_element_type=jnp.float32
+    )
+
+
+def fast_kernel(
+    n_ctx, n_dp, scale,
+    values, grads, fhi_h, flo_h, ihi_h, ilo_h, w_first, sine_freq, w_inner, w_last, decay, feat,
+    out_first, out_inner, out_last,
+    tokens, fhi, flo, ihi, ilo, window, lagged, small, partial, quarter, rx, columns, every,
+    tab_sem, own_sem, s1, r1, s2, r2, s3, r3, s4, r4,
+):
+    me = lax.axis_index("ctx")
+    md = lax.axis_index("dp")
+    block, width = values.shape[1], values.shape[2] // n_ctx
+    total = block * n_ctx
+    hidden = w_inner.shape[0]
+    part = hidden // n_dp
+
+    def ctx_of(k):
+        return lax.rem(me + k, n_ctx)
+
+    def dp_of(k):
+        return lax.rem(md + k, n_dp)
+
+    tabs = [
+        pltpu.make_async_copy(src, dst, tab_sem.at[i])
+        for i, (src, dst) in enumerate(
+            ((fhi_h, fhi), (flo_h, flo), (ihi_h, ihi), (ilo_h, ilo)))
+    ]
+    for copy in tabs:
+        copy.start()
+    my_rows = pl.ds(pl.multiple_of(me * block, block), block)
+    my_cols = pl.ds(pl.multiple_of(me * width, width), width)
+    own = [
+        pltpu.make_async_copy(
+            src.at[0, :, my_cols], tokens.at[my_rows, pl.ds(i * width, width)], own_sem.at[i])
+        for i, src in enumerate((values, grads))
+    ]
+    for copy in own:
+        copy.start()
+
+    barrier = pltpu.get_barrier_semaphore()
+    for k in range(1, n_ctx):
+        pl.semaphore_signal(
+            barrier, inc=1, device_id={"ctx": ctx_of(k)}, device_id_type=MESH)
+    for k in range(1, n_dp):
+        pl.semaphore_signal(barrier, inc=1, device_id={"dp": dp_of(k)}, device_id_type=MESH)
+    pl.semaphore_wait(barrier, n_ctx + n_dp - 2)
+
+    moves = []
+    for k in range(1, n_ctx):
+        to = ctx_of(k)
+        cols = pl.ds(pl.multiple_of(to * width, width), width)
+        for i, src in enumerate((values, grads)):
+            move = pltpu.make_async_remote_copy(
+                src_ref=src.at[0, :, cols],
+                dst_ref=tokens.at[my_rows, pl.ds(i * width, width)],
+                send_sem=s1.at[2 * k + i], recv_sem=r1.at[2 * k + i],
+                device_id={"ctx": to}, device_id_type=MESH)
+            move.start()
+            moves.append(move)
+
+    small[...] = jnp.zeros_like(small)
+    small[0:hidden, 0:hidden] = w_inner[...]
+    small[hidden:hidden + w_first.shape[0], 0:hidden] = w_first[...]
+    small[hidden + 8:hidden + 9, 0:hidden] = sine_freq[...]
+    turned = small[...].T
+    freq = turned[0:hidden, hidden + 8:hidden + 9]
+    pre = turned[0:hidden, hidden:hidden + 1] * feat[0:1, :]
+    for e in range(1, w_first.shape[0]):
+        pre = pre + turned[0:hidden, hidden + e:hidden + e + 1] * feat[e:e + 1, :]
+    act_first, slope_first = sin_cos(freq * pre)
+    act_inner, slope_inner = sin_cos(
+        freq * dot(turned[0:hidden, 0:hidden], act_first, precision=HIGHEST_PREC))
+    slope_first = slope_first * freq
+    slope_inner = slope_inner * freq
+    lag = lax.broadcasted_iota(jnp.int32, (total, width), 0).astype(jnp.float32)
+    window[...] = jnp.exp(-lag * decay[:, my_cols]) * np.float32(scale / total)
+    for copy in tabs + own:
+        copy.wait()
+    for move in moves:
+        move.wait()
+
+    lagged[...] = jnp.zeros_like(lagged)
+
+    def one_chunk(i, state):
+        both = tokens[...]
+        spec = dot(fhi[i], both) + dot(flo[i], both)
+        v_cos, g_cos = spec[:FREQ_ROWS, :width], spec[:FREQ_ROWS, width:]
+        v_sin, g_sin = spec[FREQ_ROWS:, :width], spec[FREQ_ROWS:, width:]
+        cross = jnp.concatenate(
+            [g_cos * v_cos + g_sin * v_sin, g_sin * v_cos - g_cos * v_sin], axis=0)
+        high, low = split_bf16(cross)
+        lagged[...] += dot(ihi[i], high) + dot(ihi[i], low) + dot(ilo[i], high)
+        return state
+
+    lax.fori_loop(0, total // FREQ_ROWS, one_chunk, 0)
+    cot = lagged[...] * window[...]
+    partial[:, 0:width] = dot(act_inner, cot, precision=HIGHEST_PREC)
+    grad_act = dot(w_last[:, my_cols], cot, ((1,), (1,)), HIGHEST_PREC)
+    grad_pre = grad_act * slope_inner
+    partial[:, width:width + hidden] = dot(act_first, grad_pre, ((1,), (1,)), HIGHEST_PREC)
+    grad_pre_first = dot(w_inner[...], grad_pre, precision=HIGHEST_PREC) * slope_first
+    partial[:, width + hidden:width + 2 * hidden] = dot(
+        grad_pre_first, feat[...], ((1,), (1,)), HIGHEST_PREC)
+
+    moves = []
+    for k in range(1, n_dp):
+        to = dp_of(k)
+        move = pltpu.make_async_remote_copy(
+            src_ref=partial.at[pl.ds(pl.multiple_of(to * part, part), part), :],
+            dst_ref=rx.at[k],
+            send_sem=s2.at[k], recv_sem=r2.at[k],
+            device_id={"dp": to}, device_id_type=MESH)
+        move.start()
+        moves.append(move)
+    summed = partial[pl.ds(pl.multiple_of(md * part, part), part), :]
+    for k, move in enumerate(moves):
+        move.wait_recv()
+        summed = summed + rx[k + 1]
+    quarter[...] = summed
+    gathers = []
+    for k in range(1, n_ctx):
+        move = pltpu.make_async_remote_copy(
+            src_ref=quarter, dst_ref=every.at[0, k],
+            send_sem=s3.at[k], recv_sem=r3.at[k],
+            device_id={"ctx": ctx_of(k)}, device_id_type=MESH)
+        move.start()
+        gathers.append(move)
+    every[0, 0] = summed
+    spread = []
+    for k in range(n_ctx):
+        if k:
+            gathers[k - 1].wait_recv()
+        for a in range(1, n_dp):
+            move = pltpu.make_async_remote_copy(
+                src_ref=every.at[0, k], dst_ref=every.at[a, k],
+                send_sem=s4.at[k * n_dp + a], recv_sem=r4.at[k * n_dp + a],
+                device_id={"dp": dp_of(a)}, device_id_type=MESH)
+            move.start()
+            spread.append((move, a, k))
+
+    def place(a, k):
+        rows = pl.ds(pl.multiple_of(lax.rem(md - a + n_dp, n_dp) * part, part), part)
+        cols = pl.ds(pl.multiple_of(lax.rem(me - k + n_ctx, n_ctx) * width, width), width)
+        out_last[rows, cols] = every[a, k, :, 0:width]
+        return rows
+
+    for k in range(n_ctx):
+        place(0, k)
+    for move, a, k in spread:
+        move.wait_recv()
+        place(a, k)
+    for a in range(n_dp):
+        rows = pl.ds(pl.multiple_of(lax.rem(md - a + n_dp, n_dp) * part, part), part)
+        tail = jnp.zeros((part, 2 * hidden), jnp.float32)
+        for c in range(n_ctx):
+            tail = tail + every[a, lax.rem(me - c + n_ctx, n_ctx), :, width:width + 2 * hidden]
+        columns[rows, :] = tail
+    out_inner[...] = columns[0:hidden, 0:hidden]
+    columns_t = columns[...].T
+    out_first[...] = columns_t[hidden:hidden + w_first.shape[0], 0:hidden]
+    for move in moves + gathers + [item[0] for item in spread]:
+        move.wait_send()
+
+
+def fast_shards(values, grads_out, w_first, sine_freq, w_inner, w_last, decay_rates):
+    n_ctx, n_dp = lax.axis_size("ctx"), lax.axis_size("dp")
+    block, channels = values.shape[1:]
+    total, width = block * n_ctx, channels // n_ctx
+    hidden = w_inner.shape[0]
+    part = hidden // n_dp
+    chunks = total // FREQ_ROWS
+    scale = 1.0 / math.sqrt(values.shape[0] * n_dp * total * L)
+    tables = half_step_tables(total)
+    feat = feature_rows(total, hidden)
+    anywhere = pl.BlockSpec(memory_space=pl.ANY)
+    near = pl.BlockSpec(memory_space=pltpu.VMEM)
+    f32, bf16 = jnp.float32, jnp.bfloat16
+    dma = pltpu.SemaphoreType.DMA
+    tail = width + 2 * hidden
+    return pl.pallas_call(
+        functools.partial(fast_kernel, n_ctx, n_dp, scale),
+        out_shape=(
+            jax.ShapeDtypeStruct(w_first.shape, f32),
+            jax.ShapeDtypeStruct(w_inner.shape, f32),
+            jax.ShapeDtypeStruct(w_last.shape, f32),
+        ),
+        in_specs=[anywhere] * 6 + [near] * 6,
+        out_specs=(near,) * 3,
+        scratch_shapes=[
+            pltpu.VMEM((total, 2 * width), bf16),
+            pltpu.VMEM(tables[0].shape, bf16),
+            pltpu.VMEM(tables[1].shape, bf16),
+            pltpu.VMEM(tables[2].shape, bf16),
+            pltpu.VMEM(tables[3].shape, bf16),
+            pltpu.VMEM((total, width), f32),
+            pltpu.VMEM((total, width), f32),
+            pltpu.VMEM((2 * hidden, 2 * hidden), f32),
+            pltpu.VMEM((hidden, tail), f32),
+            pltpu.VMEM((part, tail), f32),
+            pltpu.VMEM((n_dp, part, tail), f32),
+            pltpu.VMEM((hidden, 2 * hidden), f32),
+            pltpu.VMEM((n_dp, n_ctx, part, tail), f32),
+            dma((4,)), dma((2,)),
+            dma((2 * n_ctx,)), dma((2 * n_ctx,)),
+            dma((n_dp,)), dma((n_dp,)),
+            dma((n_ctx,)), dma((n_ctx,)),
+            dma((n_ctx * n_dp,)), dma((n_ctx * n_dp,)),
+        ],
+        compiler_params=pltpu.CompilerParams(
+            collective_id=0, has_side_effects=True, vmem_limit_bytes=40 * 1024 * 1024),
+        name="lag_gradients",
+    )(values, grads_out, *tables, w_first, sine_freq[None], w_inner, w_last,
+      decay_rates[None], feat)
+
+
+def fits_fast(mesh, values, w_inner, w_last):
+    n_ctx, n_dp = mesh.shape["ctx"], mesh.shape["dp"]
+    total, channels, hidden = values.shape[1], values.shape[2], w_inner.shape[0]
+    return (
+        n_ctx > 1 and n_dp > 1 and total <= min(L, 512) and total % FREQ_ROWS == 0
+        and total // n_ctx % 16 == 0 and channels % (n_ctx * 128) == 0
+        and hidden == 64 and hidden % (8 * n_dp) == 0
+        and values.shape[0] == n_dp * mesh.shape["groups"]
+    )
+
+
 def solution(mesh):
     in_specs = (
         P(("groups", "dp"), "ctx", None),
@@ -166,4 +453,11 @@
         P(),
     )
     out_specs = (P("groups", None), P("groups", None), P("groups", None))
-    return jax.shard_map(shards, mesh=mesh, in_specs=in_specs, out_specs=out_specs, check_vma=False)
+
+    def whole(values, grads_out, w_first, sine_freq, w_inner, w_last, decay_rates):
+        body = fast_shards if fits_fast(mesh, values, w_inner, w_last) else shards
+        return jax.shard_map(
+            body, mesh=mesh, in_specs=in_specs, out_specs=out_specs, check_vma=False
+        )(values, grads_out, w_first, sine_freq, w_inner, w_last, decay_rates)
+
+    return whole

time: 189 us -> 49.4 us (0.26)
  waiting for transfers between devices: 104 us -> 0 us
  matrix products: 54.2 us -> 0 us
  Pallas kernels: 0 us -> 34.8 us
  between operations: 14.2 us -> 0.66 us
  local copies, waits for them, and re-layouts: 7.91 us -> 13.3 us
  starting transfers between devices: 5.01 us -> 0 us
  other arithmetic: 3.18 us -> 0 us
    psum x1 -> x0, waiting for transfers between devices: 93.5 us -> none  [shards(): grad_act, grad_last = lax.psum((grad_act, grad_last), ('ctx', 'dp'))]
    dot_general x36 -> x0, matrix products: 54.2 us -> none  [the longest x1 7.67 us: filter_back(): jnp.dot(grad_pre, w_inner.T, precision=HIGHEST_PREC, preferred_element_ty...]
    pallas_call x0 -> x1, Pallas kernels: none -> 34.8 us  [fast_shards(): pl.pallas_call(functools.partial(fast_kernel, n_ctx, n_dp, scale), out_sh...]
    unnamed x27, local copies, waits for them, and re-layouts: 2.13 us -> 13.3 us
    all_gather x1 -> x0, waiting for transfers between devices: 9.57 us -> none  [shards(): pieces = lax.all_gather(grads_out[None], 'ctx', axis=0, tiled=True)]
    ppermute x1 -> x0, starting transfers between devices: 4.93 us -> none  [shifted(): lax.ppermute(value, axis, [(source, source + steps) for source in range(i...]
    while x24 -> x0, local copies, waits for them, and re-layouts: 4.56 us -> none
  transfers between devices with their start and end apart: 3 -> 0, of which waited for: 2 -> 0; matrix products, arithmetic and copies ran while one was open for 9% -> 0% of each run, Pallas kernels for 0% -> 0%
where the time goes in v1:
time: 49.4 us; the launch traced here: 48.8 us
  Pallas kernels  34.8 us (70%)
  local copies, waits for them, and re-layouts  13.3 us (27%)
  between operations  0.66 us (1%)
    pallas_call x1, Pallas kernels, fast_shards(): pl.pallas_call(functools.partial(fast_kernel, n_ctx, n_dp, scale), out_sh...  34.8 us
    unnamed x27, local copies, waits for them, and re-layouts  13.3 us

profile of v1, /device:TPU:0, one launch (start us, length us, event | category | flops | bytes accessed | tf_op | source)
XLA Modules:
  0.0 48.8 jit_solution(12767924648717607887)
XLA Ops:
  0.6 0.0 copy-start.11
  0.6 0.6 %copy-done.11 = f32[64]{0:T(128)S(1)} copy-done((f32[64]{0:T(128)S(1)}, f32[64]{0:T(128)}, u32[]{:S(2)}) %copy-start.11) | copy-done | bytes 280
  1.3 0.0 copy-start
  1.3 1.2 %copy-done = bf16[4,512,256]{2,1,0:T(8,128)(2,1)S(1)} copy-done((bf16[4,512,256]{2,1,0:T(8,128)(2,1)S(1)}, bf16[4,512,256]{2,1,0:T(8,128)(2,1)}, u32[]{:S(2)}) %copy-start) | copy-done | bytes 1048600
  2.5 0.0 copy-start.1
  2.5 1.2 %copy-done.1 = bf16[4,512,256]{2,1,0:T(8,128)(2,1)S(1)} copy-done((bf16[4,512,256]{2,1,0:T(8,128)(2,1)S(1)}, bf16[4,512,256]{2,1,0:T(8,128)(2,1)}, u32[]{:S(2)}) %copy-start.1) | copy-done | bytes 1048600
  3.7 0.0 copy-start.2
  3.7 1.2 %copy-done.2 = bf16[4,256,512]{2,1,0:T(8,128)(2,1)S(1)} copy-done((bf16[4,256,512]{2,1,0:T(8,128)(2,1)S(1)}, bf16[4,256,512]{2,1,0:T(8,128)(2,1)}, u32[]{:S(2)}) %copy-start.2) | copy-done | bytes 1048600
  5.0 0.0 copy-start.3
  5.0 1.2 %copy-done.3 = bf16[4,256,512]{2,1,0:T(8,128)(2,1)S(1)} copy-done((bf16[4,256,512]{2,1,0:T(8,128)(2,1)S(1)}, bf16[4,256,512]{2,1,0:T(8,128)(2,1)}, u32[]{:S(2)}) %copy-start.3) | copy-done | bytes 1048600
  6.2 0.0 copy-start.4
  6.2 0.9 %copy-done.4 = bf16[1,128,1024]{2,1,0:T(8,128)(2,1)S(1)} copy-done((bf16[1,128,1024]{2,1,0:T(8,128)(2,1)S(1)}, bf16[1,128,1024]{2,1,0:T(8,128)(2,1)}, u32[]{:S(2)}) %copy-start.4) | copy-done | bytes 262168
  7.1 0.0 copy-start.5
  7.1 0.9 %copy-done.5 = bf16[1,128,1024]{2,1,0:T(8,128)(2,1)S(1)} copy-done((bf16[1,128,1024]{2,1,0:T(8,128)(2,1)S(1)}, bf16[1,128,1024]{2,1,0:T(8,128)(2,1)}, u32[]{:S(2)}) %copy-start.5) | copy-done | bytes 262168
  8.1 0.0 copy-start.6
  8.1 0.9 %copy-done.6 = f32[64,1024]{1,0:T(8,128)S(1)} copy-done((f32[64,1024]{1,0:T(8,128)S(1)}, f32[64,1024]{1,0:T(8,128)}, u32[]{:S(2)}) %copy-start.6) | copy-done | bytes 262168
  9.0 0.0 copy-start.7
  9.0 0.9 %copy-done.7 = f32[64,512]{1,0:T(8,128)S(1)} copy-done((f32[64,512]{1,0:T(8,128)S(1)}, f32[64,512]{1,0:T(8,128)}, u32[]{:S(2)}) %copy-start.7) | copy-done | bytes 131096
  9.9 0.0 copy-start.8
  9.9 0.8 %copy-done.8 = f32[64,64]{1,0:T(8,128)S(1)} copy-done((f32[64,64]{1,0:T(8,128)S(1)}, f32[64,64]{1,0:T(8,128)}, u32[]{:S(2)}) %copy-start.8) | copy-done | bytes 16408
  10.7 0.0 copy-start.9
  10.7 0.7 %copy-done.9 = f32[5,64]{1,0:T(8,128)S(1)} copy-done((f32[5,64]{1,0:T(8,128)S(1)}, f32[5,64]{1,0:T(8,128)}, u32[]{:S(2)}) %copy-start.9) | copy-done | bytes 1304
  11.4 0.0 copy-start.10
  11.4 0.7 %copy-done.10 = f32[1024]{0:T(1024)S(1)} copy-done((f32[1024]{0:T(1024)S(1)}, f32[1024]{0:T(1024)}, u32[]{:S(2)}) %copy-start.10) | copy-done | bytes 4120
  12.1 34.8 %lag_gradients.1 = (f32[5,64]{1,0:T(8,128)S(1)}, f32[64,64]{1,0:T(8,128)S(1)}, f32[64,1024]{1,0:T(8,128)S(1)}) custom-call(bf16[1,128,1024]{2,1,0:T(8,128)(2,1)S(1)} %copy-done.4, bf16[1,128,1024]{2,1,0:T(8,128)(2,1)S(1)} %copy-done.5, bf16[4,256,512]{2,1,0:T(8,128)(2,1)S(1)} %copy-done.3, bf16[4,256,512]{2,1,0:T(8,128)(2,1)S(1)} %copy-done.2, ...), custom_call_target="tpu_custom_call" | custom-call | tf_op jit(solution)/shard_map/lag_gradients/pallas_call | solution.py:398
  46.9 0.6 %copy.18 = f32[5,64]{1,0:T(8,128)} copy(f32[5,64]{1,0:T(8,128)S(1)} %get-tuple-element.6) | data formatting | bytes 2560
  47.5 0.6 %copy.19 = f32[64,64]{1,0:T(8,128)} copy(f32[64,64]{1,0:T(8,128)S(1)} %get-tuple-element.7) | data formatting | bytes 32768
  48.1 0.7 %copy.20 = f32[64,1024]{1,0:T(8,128)} copy(f32[64,1024]{1,0:T(8,128)S(1)} %get-tuple-element.8) | data formatting | bytes 524288
Async XLA Ops:
  0.6 0.7 %copy-start.11 = (f32[64]{0:T(128)S(1)}, f32[64]{0:T(128)}, u32[]{:S(2)}) copy-start(f32[64]{0:T(128)} %param.15) | copy-start | bytes 772
  1.3 1.2 %copy-start = (bf16[4,512,256]{2,1,0:T(8,128)(2,1)S(1)}, bf16[4,512,256]{2,1,0:T(8,128)(2,1)}, u32[]{:S(2)}) copy-start(bf16[4,512,256]{2,1,0:T(8,128)(2,1)} %constant.13.clone.ilo_h) | copy-start | bytes 3145732
  2.5 1.2 %copy-start.1 = (bf16[4,512,256]{2,1,0:T(8,128)(2,1)S(1)}, bf16[4,512,256]{2,1,0:T(8,128)(2,1)}, u32[]{:S(2)}) copy-start(bf16[4,512,256]{2,1,0:T(8,128)(2,1)} %constant.12.clone.ihi_h) | copy-start | bytes 3145732
  3.7 1.2 %copy-start.2 = (bf16[4,256,512]{2,1,0:T(8,128)(2,1)S(1)}, bf16[4,256,512]{2,1,0:T(8,128)(2,1)}, u32[]{:S(2)}) copy-start(bf16[4,256,512]{2,1,0:T(8,128)(2,1)} %constant.11.clone.flo_h) | copy-start | bytes 3145732
  5.0 1.2 %copy-start.3 = (bf16[4,256,512]{2,1,0:T(8,128)(2,1)S(1)}, bf16[4,256,512]{2,1,0:T(8,128)(2,1)}, u32[]{:S(2)}) copy-start(bf16[4,256,512]{2,1,0:T(8,128)(2,1)} %constant.10.clone.fhi_h) | copy-start | bytes 3145732
  6.2 0.9 %copy-start.4 = (bf16[1,128,1024]{2,1,0:T(8,128)(2,1)S(1)}, bf16[1,128,1024]{2,1,0:T(8,128)(2,1)}, u32[]{:S(2)}) copy-start(bf16[1,128,1024]{2,1,0:T(8,128)(2,1)} %values.1) | copy-start | bytes 786436
  7.1 0.9 %copy-start.5 = (bf16[1,128,1024]{2,1,0:T(8,128)(2,1)S(1)}, bf16[1,128,1024]{2,1,0:T(8,128)(2,1)}, u32[]{:S(2)}) copy-start(bf16[1,128,1024]{2,1,0:T(8,128)(2,1)} %grads.1) | copy-start | bytes 786436
  8.1 0.9 %copy-start.6 = (f32[64,1024]{1,0:T(8,128)S(1)}, f32[64,1024]{1,0:T(8,128)}, u32[]{:S(2)}) copy-start(f32[64,1024]{1,0:T(8,128)} %w_last.1) | copy-start | bytes 786436
  9.0 0.9 %copy-start.7 = (f32[64,512]{1,0:T(8,128)S(1)}, f32[64,512]{1,0:T(8,128)}, u32[]{:S(2)}) copy-start(f32[64,512]{1,0:T(8,128)} %constant.14.clone.feat) | copy-start | bytes 393220
  9.9 0.8 %copy-start.8 = (f32[64,64]{1,0:T(8,128)S(1)}, f32[64,64]{1,0:T(8,128)}, u32[]{:S(2)}) copy-start(f32[64,64]{1,0:T(8,128)} %w_inner.1) | copy-start | bytes 49156
  10.7 0.7 %copy-start.9 = (f32[5,64]{1,0:T(8,128)S(1)}, f32[5,64]{1,0:T(8,128)}, u32[]{:S(2)}) copy-start(f32[5,64]{1,0:T(8,128)} %w_first.1) | copy-start | bytes 3844
  11.4 0.7 %copy-start.10 = (f32[1024]{0:T(1024)S(1)}, f32[1024]{0:T(1024)}, u32[]{:S(2)}) copy-start(f32[1024]{0:T(1024)} %param.18) | copy-start | bytes 12292

commit v2 on v1

--- a/solution.py
+++ b/solution.py
@@ -162,6 +162,7 @@
 
 MESH = pl.DeviceIdType.MESH
 FREQ_ROWS = 128
+VMEM_BYTES = 60 * 1024 * 1024
 
 
 def split_bf16(array):
@@ -218,11 +219,19 @@
     )
 
 
+def dot_parts(a, b, dims=((1,), (0,))):
+    rows = a[0].shape[0]
+    first = dot(jnp.concatenate(a, axis=0), b[0], dims)
+    return first[:rows] + first[rows:] + dot(a[0], b[1], dims)
+
+
 def fast_kernel(
     n_ctx, n_dp, scale,
-    values, grads, fhi_h, flo_h, ihi_h, ilo_h, w_first, sine_freq, w_inner, w_last, decay, feat,
+    values, grads, fhi_h, flo_h, ihi_h, ilo_h,
+    w_first_h, sine_freq_h, w_inner_h, w_last_h, decay_h, feat_h,
     out_first, out_inner, out_last,
-    tokens, fhi, flo, ihi, ilo, window, lagged, small, partial, quarter, rx, columns, every,
+    w_first, sine_freq, w_inner, w_last, decay, feat,
+    tokens, fhi, flo, ihi, ilo, window, small, partial, quarter, rx, columns, every,
     tab_sem, own_sem, s1, r1, s2, r2, s3, r3, s4, r4,
 ):
     me = lax.axis_index("ctx")
@@ -238,15 +247,23 @@
     def dp_of(k):
         return lax.rem(md + k, n_dp)
 
-    tabs = [
-        pltpu.make_async_copy(src, dst, tab_sem.at[i])
-        for i, (src, dst) in enumerate(
-            ((fhi_h, fhi), (flo_h, flo), (ihi_h, ihi), (ilo_h, ilo)))
-    ]
-    for copy in tabs:
-        copy.start()
+    barrier = pltpu.get_barrier_semaphore()
+    for k in range(1, n_ctx):
+        pl.semaphore_signal(
+            barrier, inc=1, device_id={"ctx": ctx_of(k)}, device_id_type=MESH)
+    for k in range(1, n_dp):
+        pl.semaphore_signal(barrier, inc=1, device_id={"dp": dp_of(k)}, device_id_type=MESH)
     my_rows = pl.ds(pl.multiple_of(me * block, block), block)
     my_cols = pl.ds(pl.multiple_of(me * width, width), width)
+    pairs = (
+        (w_first_h, w_first), (sine_freq_h, sine_freq), (w_inner_h, w_inner),
+        (decay_h.at[:, my_cols], decay), (feat_h, feat), (w_last_h.at[:, my_cols], w_last),
+        (fhi_h, fhi), (flo_h, flo), (ihi_h, ihi), (ilo_h, ilo))
+    loads = [
+        pltpu.make_async_copy(src, dst, tab_sem.at[i]) for i, (src, dst) in enumerate(pairs)]
+    for copy in loads:
+        copy.start()
+    params, tabs = loads[:6], loads[6:]
     own = [
         pltpu.make_async_copy(
             src.at[0, :, my_cols], tokens.at[my_rows, pl.ds(i * width, width)], own_sem.at[i])
@@ -255,12 +272,6 @@
     for copy in own:
         copy.start()
 
-    barrier = pltpu.get_barrier_semaphore()
-    for k in range(1, n_ctx):
-        pl.semaphore_signal(
-            barrier, inc=1, device_id={"ctx": ctx_of(k)}, device_id_type=MESH)
-    for k in range(1, n_dp):
-        pl.semaphore_signal(barrier, inc=1, device_id={"dp": dp_of(k)}, device_id_type=MESH)
     pl.semaphore_wait(barrier, n_ctx + n_dp - 2)
 
     moves = []
@@ -276,6 +287,8 @@
             move.start()
             moves.append(move)
 
+    for copy in params:
+        copy.wait()
     small[...] = jnp.zeros_like(small)
     small[0:hidden, 0:hidden] = w_inner[...]
     small[hidden:hidden + w_first.shape[0], 0:hidden] = w_first[...]
@@ -288,37 +301,38 @@
     act_first, slope_first = sin_cos(freq * pre)
     act_inner, slope_inner = sin_cos(
         freq * dot(turned[0:hidden, 0:hidden], act_first, precision=HIGHEST_PREC))
+    act_inner_parts, act_first_parts = split_bf16(act_inner), split_bf16(act_first)
+    w_last_parts, w_inner_parts = split_bf16(w_last[...]), split_bf16(w_inner[...])
+    feat_parts = split_bf16(feat[...])
     slope_first = slope_first * freq
     slope_inner = slope_inner * freq
     lag = lax.broadcasted_iota(jnp.int32, (total, width), 0).astype(jnp.float32)
-    window[...] = jnp.exp(-lag * decay[:, my_cols]) * np.float32(scale / total)
+    window[...] = jnp.exp(-lag * decay[...]) * np.float32(scale / total)
     for copy in tabs + own:
         copy.wait()
     for move in moves:
         move.wait()
 
-    lagged[...] = jnp.zeros_like(lagged)
-
-    def one_chunk(i, state):
-        both = tokens[...]
+    both = tokens[...]
+    lagged = None
+    for i in range(total // FREQ_ROWS):
         spec = dot(fhi[i], both) + dot(flo[i], both)
         v_cos, g_cos = spec[:FREQ_ROWS, :width], spec[:FREQ_ROWS, width:]
         v_sin, g_sin = spec[FREQ_ROWS:, :width], spec[FREQ_ROWS:, width:]
         cross = jnp.concatenate(
             [g_cos * v_cos + g_sin * v_sin, g_sin * v_cos - g_cos * v_sin], axis=0)
         high, low = split_bf16(cross)
-        lagged[...] += dot(ihi[i], high) + dot(ihi[i], low) + dot(ilo[i], high)
-        return state
-
-    lax.fori_loop(0, total // FREQ_ROWS, one_chunk, 0)
-    cot = lagged[...] * window[...]
-    partial[:, 0:width] = dot(act_inner, cot, precision=HIGHEST_PREC)
-    grad_act = dot(w_last[:, my_cols], cot, ((1,), (1,)), HIGHEST_PREC)
-    grad_pre = grad_act * slope_inner
-    partial[:, width:width + hidden] = dot(act_first, grad_pre, ((1,), (1,)), HIGHEST_PREC)
-    grad_pre_first = dot(w_inner[...], grad_pre, precision=HIGHEST_PREC) * slope_first
-    partial[:, width + hidden:width + 2 * hidden] = dot(
-        grad_pre_first, feat[...], ((1,), (1,)), HIGHEST_PREC)
+        update = dot(ihi[i], high) + dot(ihi[i], low) + dot(ilo[i], high)
+        lagged = update if lagged is None else lagged + update
+    cot = split_bf16(lagged * window[...])
+    across = ((1,), (1,))
+    partial[:, 0:width] = dot_parts(act_inner_parts, cot)
+    grad_pre = dot_parts(w_last_parts, cot, across) * slope_inner
+    grad_parts = split_bf16(grad_pre)
+    partial[:, width:width + hidden] = dot_parts(act_first_parts, grad_parts, across)
+    grad_pre_first = dot_parts(w_inner_parts, grad_parts) * slope_first
+    partial[:, width + hidden:width + 2 * hidden] = dot_parts(
+        split_bf16(grad_pre_first), feat_parts, across)
 
     moves = []
     for k in range(1, n_dp):
@@ -402,15 +416,20 @@
             jax.ShapeDtypeStruct(w_inner.shape, f32),
             jax.ShapeDtypeStruct(w_last.shape, f32),
         ),
-        in_specs=[anywhere] * 6 + [near] * 6,
+        in_specs=[anywhere] * 12,
         out_specs=(near,) * 3,
         scratch_shapes=[
+            pltpu.VMEM(w_first.shape, f32),
+            pltpu.VMEM((1, hidden), f32),
+            pltpu.VMEM(w_inner.shape, f32),
+            pltpu.VMEM((hidden, width), f32),
+            pltpu.VMEM((1, width), f32),
+            pltpu.VMEM(feat.shape, f32),
             pltpu.VMEM((total, 2 * width), bf16),
             pltpu.VMEM(tables[0].shape, bf16),
             pltpu.VMEM(tables[1].shape, bf16),
             pltpu.VMEM(tables[2].shape, bf16),
             pltpu.VMEM(tables[3].shape, bf16),
-            pltpu.VMEM((total, width), f32),
             pltpu.VMEM((total, width), f32),
             pltpu.VMEM((2 * hidden, 2 * hidden), f32),
             pltpu.VMEM((hidden, tail), f32),
@@ -418,14 +437,14 @@
             pltpu.VMEM((n_dp, part, tail), f32),
             pltpu.VMEM((hidden, 2 * hidden), f32),
             pltpu.VMEM((n_dp, n_ctx, part, tail), f32),
-            dma((4,)), dma((2,)),
+            dma((10,)), dma((2,)),
             dma((2 * n_ctx,)), dma((2 * n_ctx,)),
             dma((n_dp,)), dma((n_dp,)),
             dma((n_ctx,)), dma((n_ctx,)),
             dma((n_ctx * n_dp,)), dma((n_ctx * n_dp,)),
         ],
         compiler_params=pltpu.CompilerParams(
-            collective_id=0, has_side_effects=True, vmem_limit_bytes=40 * 1024 * 1024),
+            collective_id=0, has_side_effects=True, vmem_limit_bytes=VMEM_BYTES),
         name="lag_gradients",
     )(values, grads_out, *tables, w_first, sine_freq[None], w_inner, w_last,
       decay_rates[None], feat)

time: 49.4 us -> 39.2 us (0.79)
  local copies, waits for them, and re-layouts: 13.3 us -> 4.31 us
  Pallas kernels: 34.8 us -> 34 us
    unnamed x27 -> x5, local copies, waits for them, and re-layouts: 13.3 us -> 4.31 us
    pallas_call x1, Pallas kernels: 34.8 us -> 34 us  [fast_shards(): pl.pallas_call(functools.partial(fast_kernel, n_ctx, n_dp, scale), out_sh...]
where the time goes in v2:
time: 39.2 us; the launch traced here: 39 us
  Pallas kernels  34 us (87%)
  local copies, waits for them, and re-layouts  4.31 us (11%)
  between operations  0.65 us (2%)
    pallas_call x1, Pallas kernels, fast_shards(): pl.pallas_call(functools.partial(fast_kernel, n_ctx, n_dp, scale), out_sh...  34 us
    unnamed x5, local copies, waits for them, and re-layouts  4.31 us

profile of v2, /device:TPU:0, one launch (start us, length us, event | category | flops | bytes accessed | tf_op | source)
XLA Modules:
  0.0 39.0 jit_solution(14820054187118058370)
XLA Ops:
  0.6 34.0 %lag_gradients.1 = (f32[5,64]{1,0:T(8,128)}, f32[64,64]{1,0:T(8,128)}, f32[64,1024]{1,0:T(8,128)}) custom-call(bf16[1,128,1024]{2,1,0:T(8,128)(2,1)} %values.1, bf16[1,128,1024]{2,1,0:T(8,128)(2,1)} %grads.1, bf16[4,256,512]{2,1,0:T(8,128)(2,1)} %constant.10.clone.fhi_h, bf16[4,256,512]{2,1,0:T(8,128)(2,1)} %constant.11.clone.flo_h, ...), custom_call_target="tpu_custom_call" | custom-call | tf_op jit(solution)/shard_map/lag_gradients/pallas_call | solution.py:412
  34.7 0.0 copy-start
  34.7 0.7 %copy-done = f32[5,64]{1,0:T(8,128)S(1)} copy-done((f32[5,64]{1,0:T(8,128)S(1)}, f32[5,64]{1,0:T(8,128)}, u32[]{:S(2)}) %copy-start) | copy-done | bytes 1304
  35.3 0.6 %copy.18 = f32[5,64]{1,0:T(8,128)} copy(f32[5,64]{1,0:T(8,128)S(1)} %copy-done) | data formatting | bytes 2560
  35.9 1.4 %copy.19 = f32[64,64]{1,0:T(8,128)} copy(f32[64,64]{1,0:T(8,128)} %get-tuple-element.7) | data formatting | bytes 32768
  37.3 1.7 %copy.20 = f32[64,1024]{1,0:T(8,128)} copy(f32[64,1024]{1,0:T(8,128)} %get-tuple-element.8) | data formatting | bytes 524288
Async XLA Ops:
  34.7 0.7 %copy-start = (f32[5,64]{1,0:T(8,128)S(1)}, f32[5,64]{1,0:T(8,128)}, u32[]{:S(2)}) copy-start(f32[5,64]{1,0:T(8,128)} %get-tuple-element.6) | copy-start | bytes 3844

commit v3 on v2

--- a/solution.py
+++ b/solution.py
@@ -231,7 +231,7 @@
     w_first_h, sine_freq_h, w_inner_h, w_last_h, decay_h, feat_h,
     out_first, out_inner, out_last,
     w_first, sine_freq, w_inner, w_last, decay, feat,
-    tokens, fhi, flo, ihi, ilo, window, small, partial, quarter, rx, columns, every,
+    tokens, fhi, flo, ihi, ilo, window, small, partial, rx, columns, landed, every, tails, spectra,
     tab_sem, own_sem, s1, r1, s2, r2, s3, r3, s4, r4,
 ):
     me = lax.axis_index("ctx")
@@ -275,10 +275,10 @@
     pl.semaphore_wait(barrier, n_ctx + n_dp - 2)
 
     moves = []
-    for k in range(1, n_ctx):
-        to = ctx_of(k)
-        cols = pl.ds(pl.multiple_of(to * width, width), width)
-        for i, src in enumerate((values, grads)):
+    for i, src in enumerate((values, grads)):
+        for k in (2, 1, 3) if n_ctx == 4 else range(1, n_ctx):
+            to = ctx_of(k)
+            cols = pl.ds(pl.multiple_of(to * width, width), width)
             move = pltpu.make_async_remote_copy(
                 src_ref=src.at[0, :, cols],
                 dst_ref=tokens.at[my_rows, pl.ds(i * width, width)],
@@ -310,15 +310,21 @@
     window[...] = jnp.exp(-lag * decay[...]) * np.float32(scale / total)
     for copy in tabs + own:
         copy.wait()
-    for move in moves:
-        move.wait()
-
-    both = tokens[...]
+    sent, moves = moves, None
+    for move in sent[:n_ctx - 1]:
+        move.wait_recv()
+    held = tokens[:, :width]
+    for i in range(total // FREQ_ROWS):
+        spectra[i] = dot(fhi[i], held) + dot(flo[i], held)
+    for move in sent[n_ctx - 1:]:
+        move.wait_recv()
+
+    held = tokens[:, width:]
     lagged = None
     for i in range(total // FREQ_ROWS):
-        spec = dot(fhi[i], both) + dot(flo[i], both)
-        v_cos, g_cos = spec[:FREQ_ROWS, :width], spec[:FREQ_ROWS, width:]
-        v_sin, g_sin = spec[FREQ_ROWS:, :width], spec[FREQ_ROWS:, width:]
+        spec = dot(fhi[i], held) + dot(flo[i], held)
+        v_cos, v_sin = spectra[i, :FREQ_ROWS], spectra[i, FREQ_ROWS:]
+        g_cos, g_sin = spec[:FREQ_ROWS], spec[FREQ_ROWS:]
         cross = jnp.concatenate(
             [g_cos * v_cos + g_sin * v_sin, g_sin * v_cos - g_cos * v_sin], axis=0)
         high, low = split_bf16(cross)
@@ -348,50 +354,73 @@
     for k, move in enumerate(moves):
         move.wait_recv()
         summed = summed + rx[k + 1]
-    quarter[...] = summed
+    landed[0] = summed
     gathers = []
     for k in range(1, n_ctx):
         move = pltpu.make_async_remote_copy(
-            src_ref=quarter, dst_ref=every.at[0, k],
+            src_ref=landed.at[0], dst_ref=landed.at[k],
             send_sem=s3.at[k], recv_sem=r3.at[k],
             device_id={"ctx": ctx_of(k)}, device_id_type=MESH)
         move.start()
         gathers.append(move)
-    every[0, 0] = summed
-    spread = []
+
+    mate = md + 1 - 2 * lax.rem(md, 2)
+    far = lax.rem(md + 2, 4)
+    rows_of = [
+        pl.ds(pl.multiple_of(q * part, part), part)
+        for q in (md, mate, far, lax.rem(mate + 2, 4))]
+
+    def pass_on(src, dst, k, a):
+        move = pltpu.make_async_remote_copy(
+            src_ref=src, dst_ref=dst, send_sem=s4.at[4 * k + a], recv_sem=r4.at[4 * k + a],
+            device_id={"dp": far if a == 2 else mate}, device_id_type=MESH)
+        move.start()
+        return move
+
+    def place(block, a, k):
+        cols = pl.ds(pl.multiple_of(lax.rem(me - k + n_ctx, n_ctx) * width, width), width)
+        out_last[rows_of[a], cols] = block
+
+    spread = [[None] * 4 for _ in range(n_ctx + 1)]
     for k in range(n_ctx):
         if k:
             gathers[k - 1].wait_recv()
-        for a in range(1, n_dp):
-            move = pltpu.make_async_remote_copy(
-                src_ref=every.at[0, k], dst_ref=every.at[a, k],
-                send_sem=s4.at[k * n_dp + a], recv_sem=r4.at[k * n_dp + a],
-                device_id={"dp": dp_of(a)}, device_id_type=MESH)
-            move.start()
-            spread.append((move, a, k))
-
-    def place(a, k):
-        rows = pl.ds(pl.multiple_of(lax.rem(md - a + n_dp, n_dp) * part, part), part)
-        cols = pl.ds(pl.multiple_of(lax.rem(me - k + n_ctx, n_ctx) * width, width), width)
-        out_last[rows, cols] = every[a, k, :, 0:width]
-        return rows
-
+        for a in (2, 1):
+            spread[k][a] = pass_on(landed.at[k, :, 0:width], every.at[a, k], k, a)
+    tail = jnp.zeros((part, 2 * hidden), jnp.float32)
+    for c in range(n_ctx):
+        tail = tail + landed[lax.rem(me - c + n_ctx, n_ctx), :, width:width + 2 * hidden]
+    tails[0] = tail
+    for a in (2, 1):
+        spread[n_ctx][a] = pass_on(tails.at[0], tails.at[a], n_ctx, a)
     for k in range(n_ctx):
-        place(0, k)
-    for move, a, k in spread:
-        move.wait_recv()
-        place(a, k)
-    for a in range(n_dp):
-        rows = pl.ds(pl.multiple_of(lax.rem(md - a + n_dp, n_dp) * part, part), part)
-        tail = jnp.zeros((part, 2 * hidden), jnp.float32)
-        for c in range(n_ctx):
-            tail = tail + every[a, lax.rem(me - c + n_ctx, n_ctx), :, width:width + 2 * hidden]
-        columns[rows, :] = tail
+        spread[k][2].wait_recv()
+        spread[k][3] = pass_on(every.at[2, k], every.at[3, k], k, 3)
+    spread[n_ctx][2].wait_recv()
+    spread[n_ctx][3] = pass_on(tails.at[2], tails.at[3], n_ctx, 3)
+    for k in range(n_ctx):
+        place(landed[k, :, 0:width], 0, k)
+        place(every[2, k], 2, k)
+        spread[k][1].wait_recv()
+        place(every[1, k], 1, k)
+    for k in range(n_ctx):
+        spread[k][3].wait_recv()
+        place(every[3, k], 3, k)
+    spread[n_ctx][1].wait_recv()
+    spread[n_ctx][3].wait_recv()
+    for a in range(4):
+        columns[rows_of[a], :] = tails[a]
     out_inner[...] = columns[0:hidden, 0:hidden]
     columns_t = columns[...].T
     out_first[...] = columns_t[hidden:hidden + w_first.shape[0], 0:hidden]
-    for move in moves + gathers + [item[0] for item in spread]:
+    for move in sent + moves + gathers + [move for row in spread for move in row[1:]]:
         move.wait_send()
+
+
+def finish_kernel(a, b, c, out_a, out_b, out_c):
+    out_a[...] = a[...]
+    out_b[...] = b[...]
+    out_c[...] = c[...]
 
 
 def fast_shards(values, grads_out, w_first, sine_freq, w_inner, w_last, decay_rates):
@@ -409,13 +438,11 @@
     f32, bf16 = jnp.float32, jnp.bfloat16
     dma = pltpu.SemaphoreType.DMA
     tail = width + 2 * hidden
-    return pl.pallas_call(
+    out_shape = tuple(
+        jax.ShapeDtypeStruct(array.shape, f32) for array in (w_first, w_inner, w_last))
+    sums = pl.pallas_call(
         functools.partial(fast_kernel, n_ctx, n_dp, scale),
-        out_shape=(
-            jax.ShapeDtypeStruct(w_first.shape, f32),
-            jax.ShapeDtypeStruct(w_inner.shape, f32),
-            jax.ShapeDtypeStruct(w_last.shape, f32),
-        ),
+        out_shape=out_shape,
         in_specs=[anywhere] * 12,
         out_specs=(near,) * 3,
         scratch_shapes=[
@@ -433,28 +460,38 @@
             pltpu.VMEM((total, width), f32),
             pltpu.VMEM((2 * hidden, 2 * hidden), f32),
             pltpu.VMEM((hidden, tail), f32),
-            pltpu.VMEM((part, tail), f32),
             pltpu.VMEM((n_dp, part, tail), f32),
             pltpu.VMEM((hidden, 2 * hidden), f32),
-            pltpu.VMEM((n_dp, n_ctx, part, tail), f32),
+            pltpu.VMEM((n_ctx, part, tail), f32),
+            pltpu.VMEM((4, n_ctx, part, width), f32),
+            pltpu.VMEM((4, part, 2 * hidden), f32),
+            pltpu.VMEM((chunks, 2 * FREQ_ROWS, width), f32),
             dma((10,)), dma((2,)),
             dma((2 * n_ctx,)), dma((2 * n_ctx,)),
             dma((n_dp,)), dma((n_dp,)),
             dma((n_ctx,)), dma((n_ctx,)),
-            dma((n_ctx * n_dp,)), dma((n_ctx * n_dp,)),
+            dma((4 * n_ctx + 4,)), dma((4 * n_ctx + 4,)),
         ],
         compiler_params=pltpu.CompilerParams(
             collective_id=0, has_side_effects=True, vmem_limit_bytes=VMEM_BYTES),
         name="lag_gradients",
     )(values, grads_out, *tables, w_first, sine_freq[None], w_inner, w_last,
       decay_rates[None], feat)
+    return pl.pallas_call(
+        finish_kernel,
+        out_shape=out_shape,
+        in_specs=[near] * 3,
+        out_specs=(near,) * 3,
+        compiler_params=pltpu.CompilerParams(vmem_limit_bytes=60 * 1024 * 1024),
+        name="hand_over",
+    )(*sums)
 
 
 def fits_fast(mesh, values, w_inner, w_last):
     n_ctx, n_dp = mesh.shape["ctx"], mesh.shape["dp"]
     total, channels, hidden = values.shape[1], values.shape[2], w_inner.shape[0]
     return (
-        n_ctx > 1 and n_dp > 1 and total <= min(L, 512) and total % FREQ_ROWS == 0
+        n_ctx > 1 and n_dp == 4 and total <= min(L, 512) and total % FREQ_ROWS == 0
         and total // n_ctx % 16 == 0 and channels % (n_ctx * 128) == 0
         and hidden == 64 and hidden % (8 * n_dp) == 0
         and values.shape[0] == n_dp * mesh.shape["groups"]

time: 39.2 us -> 35.6 us (0.908)
  local copies, waits for them, and re-layouts: 4.31 us -> 0 us
  Pallas kernels: 34 us -> 34.8 us
    unnamed x5 -> x0, local copies, waits for them, and re-layouts: 4.31 us -> none
    pallas_call x0 -> x1, Pallas kernels: none -> 1.7 us  [fast_shards(): pl.pallas_call(finish_kernel, out_shape=out_shape, in_specs=[near] * 3, o...]
    pallas_call x1, Pallas kernels: 34 us -> 33.1 us  [fast_shards(): pl.pallas_call(functools.partial(fast_kernel, n_ctx, n_dp, scale), out_sh...]
where the time goes in v3:
time: 35.6 us; the launch traced here: 35.4 us
  Pallas kernels  34.8 us (98%)
  between operations  0.64 us (2%)
    pallas_call x1, Pallas kernels, fast_shards(): pl.pallas_call(functools.partial(fast_kernel, n_ctx, n_dp, scale), out_sh...  33.1 us
    pallas_call x1, Pallas kernels, fast_shards(): pl.pallas_call(finish_kernel, out_shape=out_shape, in_specs=[near] * 3, o...  1.7 us

profile of v3, /device:TPU:0, one launch (start us, length us, event | category | flops | bytes accessed | tf_op | source)
XLA Modules:
  0.0 35.4 jit_solution(8463332537739353652)
XLA Ops:
  0.6 33.1 %lag_gradients.1 = (f32[5,64]{1,0:T(8,128)}, f32[64,64]{1,0:T(8,128)}, f32[64,1024]{1,0:T(8,128)}) custom-call(bf16[1,128,1024]{2,1,0:T(8,128)(2,1)} %values.1, bf16[1,128,1024]{2,1,0:T(8,128)(2,1)} %grads.1, bf16[4,256,512]{2,1,0:T(8,128)(2,1)} %constant.10.clone.fhi_h, bf16[4,256,512]{2,1,0:T(8,128)(2,1)} %constant.11.clone.flo_h, ...), custom_call_target="tpu_custom_call" | custom-call | tf_op jit(solution)/shard_map/lag_gradients/pallas_call | solution.py:443
  33.7 1.7 %hand_over.1 = (f32[5,64]{1,0:T(8,128)}, f32[64,64]{1,0:T(8,128)}, f32[64,1024]{1,0:T(8,128)}) custom-call(f32[5,64]{1,0:T(8,128)} %get-tuple-element.6.a, f32[64,64]{1,0:T(8,128)} %get-tuple-element.7.b, f32[64,1024]{1,0:T(8,128)} %get-tuple-element.8.c), custom_call_target="tpu_custom_call" | custom-call | tf_op jit(solution)/shard_map/hand_over/pallas_call | solution.py:480

commit v4 on v3

--- a/solution.py
+++ b/solution.py
@@ -261,9 +261,9 @@
         (fhi_h, fhi), (flo_h, flo), (ihi_h, ihi), (ilo_h, ilo))
     loads = [
         pltpu.make_async_copy(src, dst, tab_sem.at[i]) for i, (src, dst) in enumerate(pairs)]
-    for copy in loads:
+    params, tabs = loads[:6], loads[6:]
+    for copy in params:
         copy.start()
-    params, tabs = loads[:6], loads[6:]
     own = [
         pltpu.make_async_copy(
             src.at[0, :, my_cols], tokens.at[my_rows, pl.ds(i * width, width)], own_sem.at[i])
@@ -286,6 +286,9 @@
                 device_id={"ctx": to}, device_id_type=MESH)
             move.start()
             moves.append(move)
+
+    for copy in tabs:
+        copy.start()
 
     for copy in params:
         copy.wait()
@@ -332,37 +335,45 @@
         lagged = update if lagged is None else lagged + update
     cot = split_bf16(lagged * window[...])
     across = ((1,), (1,))
+    lanes = (pl.ds(0, width), pl.ds(width, 2 * hidden))
+    moves, gathers = [[], []], [[], []]
+
+    def send_rows(i):
+        for k in range(1, n_dp):
+            to = dp_of(k)
+            move = pltpu.make_async_remote_copy(
+                src_ref=partial.at[pl.ds(pl.multiple_of(to * part, part), part), lanes[i]],
+                dst_ref=rx.at[k, :, lanes[i]],
+                send_sem=s2.at[i * n_dp + k], recv_sem=r2.at[i * n_dp + k],
+                device_id={"dp": to}, device_id_type=MESH)
+            move.start()
+            moves[i].append(move)
+
+    def add_and_gather(i):
+        summed = partial[pl.ds(pl.multiple_of(md * part, part), part), lanes[i]]
+        for k, move in enumerate(moves[i]):
+            move.wait_recv()
+            summed = summed + rx[k + 1, :, lanes[i]]
+        landed[0, :, lanes[i]] = summed
+        for k in range(1, n_ctx):
+            move = pltpu.make_async_remote_copy(
+                src_ref=landed.at[0, :, lanes[i]], dst_ref=landed.at[k, :, lanes[i]],
+                send_sem=s3.at[i * n_ctx + k], recv_sem=r3.at[i * n_ctx + k],
+                device_id={"ctx": ctx_of(k)}, device_id_type=MESH)
+            move.start()
+            gathers[i].append(move)
+
     partial[:, 0:width] = dot_parts(act_inner_parts, cot)
+    send_rows(0)
     grad_pre = dot_parts(w_last_parts, cot, across) * slope_inner
     grad_parts = split_bf16(grad_pre)
     partial[:, width:width + hidden] = dot_parts(act_first_parts, grad_parts, across)
     grad_pre_first = dot_parts(w_inner_parts, grad_parts) * slope_first
     partial[:, width + hidden:width + 2 * hidden] = dot_parts(
         split_bf16(grad_pre_first), feat_parts, across)
-
-    moves = []
-    for k in range(1, n_dp):
-        to = dp_of(k)
-        move = pltpu.make_async_remote_copy(
-            src_ref=partial.at[pl.ds(pl.multiple_of(to * part, part), part), :],
-            dst_ref=rx.at[k],
-            send_sem=s2.at[k], recv_sem=r2.at[k],
-            device_id={"dp": to}, device_id_type=MESH)
-        move.start()
-        moves.append(move)
-    summed = partial[pl.ds(pl.multiple_of(md * part, part), part), :]
-    for k, move in enumerate(moves):
-        move.wait_recv()
-        summed = summed + rx[k + 1]
-    landed[0] = summed
-    gathers = []
-    for k in range(1, n_ctx):
-        move = pltpu.make_async_remote_copy(
-            src_ref=landed.at[0], dst_ref=landed.at[k],
-            send_sem=s3.at[k], recv_sem=r3.at[k],
-            device_id={"ctx": ctx_of(k)}, device_id_type=MESH)
-        move.start()
-        gathers.append(move)
+    send_rows(1)
+    add_and_gather(0)
+    add_and_gather(1)
 
     mate = md + 1 - 2 * lax.rem(md, 2)
     far = lax.rem(md + 2, 4)
@@ -384,9 +395,11 @@
     spread = [[None] * 4 for _ in range(n_ctx + 1)]
     for k in range(n_ctx):
         if k:
-            gathers[k - 1].wait_recv()
+            gathers[0][k - 1].wait_recv()
         for a in (2, 1):
             spread[k][a] = pass_on(landed.at[k, :, 0:width], every.at[a, k], k, a)
+    for move in gathers[1]:
+        move.wait_recv()
     tail = jnp.zeros((part, 2 * hidden), jnp.float32)
     for c in range(n_ctx):
         tail = tail + landed[lax.rem(me - c + n_ctx, n_ctx), :, width:width + 2 * hidden]
@@ -413,7 +426,7 @@
     out_inner[...] = columns[0:hidden, 0:hidden]
     columns_t = columns[...].T
     out_first[...] = columns_t[hidden:hidden + w_first.shape[0], 0:hidden]
-    for move in sent + moves + gathers + [move for row in spread for move in row[1:]]:
+    for move in sent + moves[0] + moves[1] + gathers[0] + gathers[1] + [move for row in spread for move in row[1:]]:
         move.wait_send()
 
 
@@ -468,8 +481,8 @@
             pltpu.VMEM((chunks, 2 * FREQ_ROWS, width), f32),
             dma((10,)), dma((2,)),
             dma((2 * n_ctx,)), dma((2 * n_ctx,)),
-            dma((n_dp,)), dma((n_dp,)),
-            dma((n_ctx,)), dma((n_ctx,)),
+            dma((2 * n_dp,)), dma((2 * n_dp,)),
+            dma((2 * n_ctx,)), dma((2 * n_ctx,)),
             dma((4 * n_ctx + 4,)), dma((4 * n_ctx + 4,)),
         ],
         compiler_params=pltpu.CompilerParams(

time: 35.6 us -> 35.1 us (0.986)
  Pallas kernels: 34.8 us -> 34.3 us
    pallas_call x1, Pallas kernels: 33.1 us -> 32.6 us  [fast_shards(): pl.pallas_call(functools.partial(fast_kernel, n_ctx, n_dp, scale), out_sh...]
where the time goes in v4:
time: 35.1 us; the launch traced here: 34.9 us
  Pallas kernels  34.3 us (98%)
  between operations  0.64 us (2%)
    pallas_call x1, Pallas kernels, fast_shards(): pl.pallas_call(functools.partial(fast_kernel, n_ctx, n_dp, scale), out_sh...  32.6 us
    pallas_call x1, Pallas kernels, fast_shards(): pl.pallas_call(finish_kernel, out_shape=out_shape, in_specs=[near] * 3, o...  1.7 us

profile of v4, /device:TPU:0, one launch (start us, length us, event | category | flops | bytes accessed | tf_op | source)
XLA Modules:
  0.0 34.9 jit_solution(9631863285707994497)
XLA Ops:
  0.6 32.6 %lag_gradients.1 = (f32[5,64]{1,0:T(8,128)}, f32[64,64]{1,0:T(8,128)}, f32[64,1024]{1,0:T(8,128)}) custom-call(bf16[1,128,1024]{2,1,0:T(8,128)(2,1)} %values.1, bf16[1,128,1024]{2,1,0:T(8,128)(2,1)} %grads.1, bf16[4,256,512]{2,1,0:T(8,128)(2,1)} %constant.10.clone.fhi_h, bf16[4,256,512]{2,1,0:T(8,128)(2,1)} %constant.11.clone.flo_h, ...), custom_call_target="tpu_custom_call" | custom-call | tf_op jit(solution)/shard_map/lag_gradients/pallas_call | solution.py:456
  33.2 1.7 %hand_over.1 = (f32[5,64]{1,0:T(8,128)}, f32[64,64]{1,0:T(8,128)}, f32[64,1024]{1,0:T(8,128)}) custom-call(f32[5,64]{1,0:T(8,128)} %get-tuple-element.6.a, f32[64,64]{1,0:T(8,128)} %get-tuple-element.7.b, f32[64,1024]{1,0:T(8,128)} %get-tuple-element.8.c), custom_call_target="tpu_custom_call" | custom-call | tf_op jit(solution)/shard_map/hand_over/pallas_call | solution.py:493

commit v5 on v4

--- a/solution.py
+++ b/solution.py
@@ -384,7 +384,7 @@
     def pass_on(src, dst, k, a):
         move = pltpu.make_async_remote_copy(
             src_ref=src, dst_ref=dst, send_sem=s4.at[4 * k + a], recv_sem=r4.at[4 * k + a],
-            device_id={"dp": far if a == 2 else mate}, device_id_type=MESH)
+            device_id={"dp": (md, mate, far, lax.rem(mate + 2, 4))[a]}, device_id_type=MESH)
         move.start()
         return move
 
@@ -396,7 +396,7 @@
     for k in range(n_ctx):
         if k:
             gathers[0][k - 1].wait_recv()
-        for a in (2, 1):
+        for a in (3, 2, 1):
             spread[k][a] = pass_on(landed.at[k, :, 0:width], every.at[a, k], k, a)
     for move in gathers[1]:
         move.wait_recv()
@@ -404,15 +404,11 @@
     for c in range(n_ctx):
         tail = tail + landed[lax.rem(me - c + n_ctx, n_ctx), :, width:width + 2 * hidden]
     tails[0] = tail
-    for a in (2, 1):
+    for a in (3, 2, 1):
         spread[n_ctx][a] = pass_on(tails.at[0], tails.at[a], n_ctx, a)
     for k in range(n_ctx):
+        place(landed[k, :, 0:width], 0, k)
         spread[k][2].wait_recv()
-        spread[k][3] = pass_on(every.at[2, k], every.at[3, k], k, 3)
-    spread[n_ctx][2].wait_recv()
-    spread[n_ctx][3] = pass_on(tails.at[2], tails.at[3], n_ctx, 3)
-    for k in range(n_ctx):
-        place(landed[k, :, 0:width], 0, k)
         place(every[2, k], 2, k)
         spread[k][1].wait_recv()
         place(every[1, k], 1, k)
@@ -420,6 +416,7 @@
         spread[k][3].wait_recv()
         place(every[3, k], 3, k)
     spread[n_ctx][1].wait_recv()
+    spread[n_ctx][2].wait_recv()
     spread[n_ctx][3].wait_recv()
     for a in range(4):
         columns[rows_of[a], :] = tails[a]

time: 35.1 us -> 34.8 us (level)
  no operation moved by 1% of the time
where the time goes in v5:
time: 34.8 us; the launch traced here: 34.7 us
  Pallas kernels  34 us (98%)
  between operations  0.64 us (2%)
    pallas_call x1, Pallas kernels, fast_shards(): pl.pallas_call(functools.partial(fast_kernel, n_ctx, n_dp, scale), out_sh...  32.3 us
    pallas_call x1, Pallas kernels, fast_shards(): pl.pallas_call(finish_kernel, out_shape=out_shape, in_specs=[near] * 3, o...  1.7 us

profile of v5, /device:TPU:0, one launch (start us, length us, event | category | flops | bytes accessed | tf_op | source)
XLA Modules:
  0.0 34.7 jit_solution(5185309425578952127)
XLA Ops:
  0.6 32.3 %lag_gradients.1 = (f32[5,64]{1,0:T(8,128)}, f32[64,64]{1,0:T(8,128)}, f32[64,1024]{1,0:T(8,128)}) custom-call(bf16[1,128,1024]{2,1,0:T(8,128)(2,1)} %values.1, bf16[1,128,1024]{2,1,0:T(8,128)(2,1)} %grads.1, bf16[4,256,512]{2,1,0:T(8,128)(2,1)} %constant.10.clone.fhi_h, bf16[4,256,512]{2,1,0:T(8,128)(2,1)} %constant.11.clone.flo_h, ...), custom_call_target="tpu_custom_call" | custom-call | tf_op jit(solution)/shard_map/lag_gradients/pallas_call | solution.py:453
  33.0 1.7 %hand_over.1 = (f32[5,64]{1,0:T(8,128)}, f32[64,64]{1,0:T(8,128)}, f32[64,1024]{1,0:T(8,128)}) custom-call(f32[5,64]{1,0:T(8,128)} %get-tuple-element.6.a, f32[64,64]{1,0:T(8,128)} %get-tuple-element.7.b, f32[64,1024]{1,0:T(8,128)} %get-tuple-element.8.c), custom_call_target="tpu_custom_call" | custom-call | tf_op jit(solution)/shard_map/hand_over/pallas_call | solution.py:490
